TPU v7x, 32 devices: a whole 2x2x4 slice. The times are simulated.
32 devices in a mesh: groups: 2 (over x), fsdp: 8 (over z, y), seq: 2 (over core).
Axes of the slice: x: 2, y: 2, z: 4, core: 2. Of those that a mesh axis runs over, the one named last changes fastest.
Arguments:
- frames: bfloat16 [16, 768, 3072], P(('groups', 'fsdp'), 'seq'), parts along dimension 0, may hold values from -6 to 6
- frozen_query_key_value: bfloat16 [3, 3072, 1536], P(None, 'fsdp', 'seq'), may hold values from -0.109375 to 0.109375
- adapter_down_weight: bfloat16 [3, 3072, 64], P(None, 'fsdp'), may hold values from -0.109375 to 0.109375
- adapter_up_weight: bfloat16 [3, 64, 1536], P(None, None, 'seq'), may hold values from -0.75 to 0.75
- query_key_norm_gain: float32 [2, 1536], P(None, 'seq'), may hold values from 0.5 to 6
Outputs:
- attended: bfloat16 [16, 768, 1536], P(('groups', 'fsdp'), 'seq'), parts along dimension 0
There are 2 independent parts, one for each index of `groups`. A program takes and returns all parts, laid end to end along the dimension named above; an argument that names none is the same for every part. Nothing has to cross between parts.
All inputs are finite; a program needn't handle non-finite values.
Results may differ from a plain program's by a relative error of at most 0.0085.
The roundings to bfloat16 on the way count: a program that leaves them out, or rounds other values in their place, can miss the bound.
Values may be sent and summed in bfloat16 or wider, within the bound.
A program may use at most 64 MiB of HBM per device.

v0:
```python
import jax
import jax.numpy as jnp
from jax import lax
from jax.sharding import PartitionSpec as P

HEAD = 128


adapter_scale = 0.5


def combined_weight_rows(frozen_weight_rows, down_rows, up_cols):
    adapter_product = jnp.einsum(
        "pnr,prc->pnc", down_rows, up_cols, preferred_element_type=jnp.float32
    )
    return (frozen_weight_rows.astype(jnp.float32) + adapter_scale * adapter_product).astype(
        jnp.bfloat16
    )


def head_norm(block, gain_rows):
    scale = lax.rsqrt(jnp.mean(block * block, axis=-1, keepdims=True) + 1e-06)
    return (block * scale * gain_rows).astype(jnp.bfloat16)


def attend(mixed, query_key_norm_gain):
    tokens = mixed.shape[1]
    heads_here = mixed.shape[2] // HEAD
    split_heads = mixed.reshape(3, tokens, heads_here, HEAD)
    gains = query_key_norm_gain.reshape(2, heads_here, HEAD)
    queries = head_norm(split_heads[0], gains[0])
    key_rows = head_norm(split_heads[1], gains[1])
    values = split_heads[2].astype(jnp.bfloat16)
    scores = jnp.einsum(
        "thd,shd->hts", queries, key_rows, preferred_element_type=jnp.float32
    ) / jnp.sqrt(jnp.float32(HEAD))
    probs = jax.nn.softmax(scores, axis=-1).astype(jnp.bfloat16)
    attended = jnp.einsum("hts,shd->thd", probs, values, preferred_element_type=jnp.float32)
    return attended.astype(jnp.bfloat16).reshape(tokens, heads_here * HEAD)


def per_device(
    frames, frozen_query_key_value, adapter_down_weight, adapter_up_weight, query_key_norm_gain
):
    whole = lax.all_gather(frames, "seq", axis=1, tiled=True)
    clip_rows = whole[0]
    merged_local = combined_weight_rows(
        frozen_query_key_value, adapter_down_weight, adapter_up_weight
    )
    combined_weight = lax.all_gather(merged_local, "fsdp", axis=1, tiled=True)
    mixed = jnp.einsum(
        "tn,pnc->ptc", clip_rows, combined_weight, preferred_element_type=jnp.float32
    )
    head_major = attend(mixed, query_key_norm_gain)
    frame_major = lax.all_to_all(head_major, "seq", split_axis=0, concat_axis=1, tiled=True)
    return frame_major[None]


def solution(mesh):
    placed = (
        P(("groups", "fsdp"), "seq", None),
        P(None, "fsdp", "seq"),
        P(None, "fsdp", None),
        P(None, None, "seq"),
        P(None, "seq"),
    )
    return jax.shard_map(
        per_device,
        mesh=mesh,
        in_specs=placed,
        out_specs=P(("groups", "fsdp"), "seq", None),
        check_vma=False,
    )
```

profile of v0, /device:TPU:0, one launch (start us, length us, event | category | flops | bytes accessed | tf_op | source)
XLA Modules:
  0.0 279.7 jit_solution(6049207141542875298)
XLA Ops:
  6.5 0.0 copy-start
  6.5 0.0 all-gather.5.cloned.1.call-start
  6.5 0.7 all-gather.5.cloned.1.call-update
  7.3 0.0 copy-start.2
  7.3 0.0 all-gather.3.cloned.1.call-start
  7.3 2.8 copy.11
  10.1 0.0 copy-done
  10.1 0.0 copy-done.2
  10.1 0.0 copy-start.3
  10.1 1.9 add_convert_fusion
  12.1 0.0 all-gather.3.cloned.1.call-update
  12.1 0.0 copy-done.3
  12.1 14.0 %all-gather.5.cloned.1.call-done = bf16[1,768,3072]{2,1,0:T(8,128)(2,1)} async-done(((bf16[1,384,3072]{2,1,0:T(8,128)(2,1)}), bf16[1,768,3072]{2,1,0:T(8,128)(2,1)}) %all-gather.5.cloned.1.call-update) | async-done | bytes 4718608 | tf_op jit(solution)/shard_map/all_gather | solution.py:45
  26.1 199.0 %all-gather.3.cloned.1.call-done = bf16[3,3072,768]{1,2,0:T(8,128)(2,1)} async-done(((bf16[3,384,768]{1,2,0:T(8,128)(2,1)}), bf16[3,3072,768]{1,2,0:T(8,128)(2,1)}) %all-gather.3.cloned.1.call-update) | async-done | bytes 14155792 | tf_op jit(solution)/shard_map/all_gather | solution.py:50
  225.1 15.4 %fusion.8 = f32[3,768,768]{1,2,0:T(8,128)S(1)} fusion(bf16[3,3072,768]{1,2,0:T(8,128)(2,1)} %all-gather.3.cloned.1.call-done, bf16[1,768,3072]{2,1,0:T(8,128)(2,1)} %all-gather.5.cloned.1.call-done), kind=kOutput, calls=%fused_computation.10 | convolution fusion | flops 10871635968 | bytes 25952256 | tf_op jit(solution)/shard_map/tn,pnc->ptc/dot_general | solution.py:51
  240.5 1.1 slice.32
  241.6 1.7 fusion.17
  243.3 3.1 %copy.12 = f32[768,6,128]{2,0,1:T(8,128)} copy(f32[768,6,128]{0,2,1:T(8,128)} %bitcast.26) | data formatting | bytes 4718592 | tf_op jit(solution)/shard_map/squeeze | solution.py:31
  246.4 1.9 multiply_reduce_fusion.2
  248.3 0.2 multiply_reduce_fusion.1
  248.5 2.0 copy.13
  250.5 0.0 copy-start.1
  250.5 9.7 %fusion.18 = (f32[6,768]{1,0:T(8,128)S(1)}, f32[6,768,768]{1,2,0:T(8,128)}) fusion(f32[768,6,128]{2,0,1:T(8,128)} %copy.12, f32[6,128]{1,0:T(8,128)S(1)} %bitcast.31, f32[768,6]{0,1:T(8,128)S(1)} %get-tuple-element.12, f32[768,6,128]{2,0,1:T(8,128)} %copy.13, f32[6,128]{1,0:T(8,128)S(1)} %bitcast.30, f32[768,6]{0,1:T(8,128)S(1)} %get-tuple-element.11), kind=kOutput, calls=%fused_computation.26 | convolution fusion | flops 920126208 | bytes 18935808 | tf_op jit(solution)/shard_map/sub | solution.py:37
  260.1 0.0 copy-done.1
  260.1 6.1 %fusion.14 = bf16[768,6,128]{0,2,1:T(8,128)(2,1)S(1)} fusion(bf16[768,6,128]{0,2,1:T(8,128)(2,1)S(1)} %bitcast.29, f32[6,768,768]{1,2,0:T(8,128)} %get-tuple-element.10, f32[6,768]{1,0:T(8,128)S(1)} %get-tuple-element.9), kind=kOutput, calls=%fused_computation.18 | convolution fusion | flops 913637376 | bytes 16533504 | tf_op jit(solution)/shard_map/hts,shd->thd/dot_general | solution.py:38
  266.3 0.3 all_to_all.12
  266.6 0.2 copy.15
  266.8 4.7 %all_to_all.16 = bf16[2,384,768]{1,2,0:T(8,128)(2,1)S(1)} all-to-all(bf16[2,384,768]{1,2,0:T(8,128)(2,1)S(1)} %copy.15), channel_id=1, replica_groups=mesh['groups'=2,'fsdp'=8,'seq'=2] {'seq'}, dimensions={0} | all-to-all | bytes 2359296 | tf_op jit(solution)/shard_map/all_to_all | solution.py:55
  271.4 1.4 copy.16
  (2 shorter events, 0.0 us)
Async XLA Ops:
  6.5 3.6 %copy-start = (bf16[3,64,768]{2,1,0:T(8,128)(2,1)S(1)}, bf16[3,64,768]{2,1,0:T(8,128)(2,1)}, u32[]{:S(2)}) copy-start(bf16[3,64,768]{2,1,0:T(8,128)(2,1)} %param.8) | copy-start | bytes 884740
  6.5 19.5 %all-gather.5.cloned.1.call-start = ((), (), s32[]{:S(2)}) async-start(), calls=%async_computation.2 | async-start | bytes 7077888 | tf_op jit(solution)/shard_map/all_gather | solution.py:45
  7.3 2.9 %copy-start.2 = (bf16[3,384,64]{1,2,0:T(8,128)(2,1)S(1)}, bf16[3,384,64]{1,2,0:T(8,128)(2,1)}, u32[]{:S(2)}) copy-start(bf16[3,384,64]{1,2,0:T(8,128)(2,1)} %param.7) | copy-start | bytes 442372
  7.3 217.8 %all-gather.3.cloned.1.call-start = ((), (), s32[]{:S(2)}) async-start(), calls=%async_computation.1 | async-start | bytes 15925248 | tf_op jit(solution)/shard_map/all_gather | solution.py:50
  10.1 2.0 copy-start.3
  250.5 9.7 %copy-start.1 = (bf16[1,768,768]{1,2,0:T(8,128)(2,1)S(1)}, bf16[1,768,768]{1,2,0:T(8,128)(2,1)}, u32[]{:S(2)}) copy-start(bf16[1,768,768]{1,2,0:T(8,128)(2,1)} %slice.32) | copy-start | bytes 3538948
Sparse Core Ops, SparseCore 0:
  8.9 17.1 all-gather.4
  28.1 196.9 all-gather.2
where the time goes:
time: 280 us
  waiting for transfers between devices  214 us (76%)
  matrix products  33.1 us (12%)
  between operations  13.5 us (5%)
  local copies, waits for them, and re-layouts  12.6 us (4%)
  blocking collectives  4.68 us (2%)
    all_gather x1, waiting for transfers between devices, per_device(): combined_weight = lax.all_gather(merged_local, 'fsdp', axis=1, tiled=True)  199 us
    dot_general x1, matrix products, per_device(): jnp.einsum('tn,pnc->ptc', clip_rows, combined_weight, preferred_element_t...  15.4 us
    all_gather x1, waiting for transfers between devices, per_device(): whole = lax.all_gather(frames, 'seq', axis=1, tiled=True)  14 us
    sub x1, matrix products, attend(): probs = jax.nn.softmax(scores, axis=-1).astype(jnp.bfloat16)  9.65 us
    dot_general x1, matrix products, attend(): jnp.einsum('hts,shd->thd', probs, values, preferred_element_type=jnp.floa...  6.13 us
  transfers between devices with their start and end apart: 2, of which 2 were waited for; matrix products, arithmetic and copies ran while one was open for 2% of the time, Pallas kernels for 0%

commit v1 on v0

v1 whole, which is shorter than its diff:
```python
import functools
import math

import jax
import jax.numpy as jnp
from jax import lax
from jax.experimental import pallas as pl
from jax.experimental.pallas import tpu as pltpu
from jax.sharding import PartitionSpec as P

HEAD = 128
MESH = pl.DeviceIdType.MESH
adapter_scale = 0.5
ROW_BLOCK = 256


def line_shape(devices):
    fast = 1
    while (fast * 2) ** 2 <= devices:
        fast *= 2
    return devices // fast, fast


def kernel(
    slow, fast, heads,
    frames, frozen, down, up, gain,
    out,
    clip_buf, weight_buf, total, out_buf, key_buf, value_buf,
    weight_send, weight_recv,
    peer_send, peer_recv, sib_send, sib_recv, fwd_send, fwd_recv, own_sem,
    out_send, out_recv, out_local,
):
    x, f, c = lax.axis_index("groups"), lax.axis_index("fsdp"), lax.axis_index("seq")
    i, j = lax.div(f, fast), lax.rem(f, fast)
    rows = frozen.shape[1]
    half = frames.shape[1]
    tokens = 2 * half
    group_rows = fast * rows
    sibling, peer, cross = (x, f, 1 - c), (1 - x, f, c), (1 - x, f, 1 - c)
    steps = {
        0: ((x, f + fast, c), i + 1 < slow),
        1: ((x, f - fast, c), i > 0),
        2: ((x, f + 1, c), j + 1 < fast),
        3: ((x, f - 1, c), j > 0),
    }

    barrier = pltpu.get_barrier_semaphore()
    for device in (sibling, peer, cross):
        pl.semaphore_signal(barrier, inc=1, device_id=device, device_id_type=MESH)
    expected = jnp.int32(3)
    for device, there in steps.values():
        expected = expected + there.astype(jnp.int32)

        @pl.when(there)
        def _(device=device):
            pl.semaphore_signal(barrier, inc=1, device_id=device, device_id_type=MESH)

    def head_columns(h):
        return pl.ds(pl.multiple_of((heads * x + h) * HEAD, HEAD), HEAD)

    def merge(h):
        for p in range(3):
            product = jnp.dot(
                down[p], up[p, :, head_columns(h)], preferred_element_type=jnp.float32
            )
            merged = frozen[p, :, head_columns(h)].astype(jnp.float32) + adapter_scale * product
            weight_buf[h, pl.ds(pl.multiple_of(f * rows, rows), rows), p * HEAD:(p + 1) * HEAD] = (
                merged.astype(jnp.bfloat16)
            )

    merge(0)
    pl.semaphore_wait(barrier, expected)

    def chunk(k):
        return pl.ds(k * group_rows, group_rows)

    def buf_rows(clip, part):
        return pl.ds(pl.multiple_of(clip * tokens + part * half, half), half)

    def own_copy(k):
        return pltpu.make_async_copy(
            frames.at[0, :, chunk(k)], clip_buf.at[buf_rows(0, c), chunk(k)], own_sem.at[k]
        )

    def sib_copy(k):
        return pltpu.make_async_remote_copy(
            src_ref=frames.at[0, :, chunk(k)],
            dst_ref=clip_buf.at[buf_rows(0, c), chunk(k)],
            send_sem=sib_send.at[k], recv_sem=sib_recv.at[k],
            device_id=sibling, device_id_type=MESH,
        )

    def peer_copy(k):
        return pltpu.make_async_remote_copy(
            src_ref=frames.at[0, :, chunk(k)],
            dst_ref=clip_buf.at[buf_rows(1, c), chunk(k)],
            send_sem=peer_send.at[k], recv_sem=peer_recv.at[k],
            device_id=peer, device_id_type=MESH,
        )

    def fwd_copy(k):
        return pltpu.make_async_remote_copy(
            src_ref=clip_buf.at[buf_rows(1, c), chunk(k)],
            dst_ref=clip_buf.at[buf_rows(1, c), chunk(k)],
            send_sem=fwd_send.at[k], recv_sem=fwd_recv.at[k],
            device_id=sibling, device_id_type=MESH,
        )

    def weight_copy(way, h, shard):
        block = weight_buf.at[h, pl.ds(pl.multiple_of(shard * rows, rows), rows), :]
        return pltpu.make_async_remote_copy(
            src_ref=block, dst_ref=block,
            send_sem=weight_send.at[way, h, shard], recv_sem=weight_recv.at[h, shard],
            device_id=steps[way][0], device_id_type=MESH,
        )

    def send(ways, h, shard):
        for way in ways:
            @pl.when(steps[way][1])
            def _(way=way):
                weight_copy(way, h, shard).start()

    def arrive(h, shard):
        weight_copy(0, h, shard).wait_recv()

    def slow_step(h, d):
        @pl.when(i - d >= 0)
        def _():
            shard = (i - d) * fast + j
            arrive(h, shard)
            send((0, 2, 3), h, shard)

        @pl.when(i + d < slow)
        def _():
            shard = (i + d) * fast + j
            arrive(h, shard)
            send((1, 2, 3), h, shard)

    def fast_line(h, k):
        def body(e, carry):
            @pl.when(j - e >= 0)
            def _():
                arrive(h, k * fast + j - e)
                if fast > 2:
                    send((2,), h, k * fast + j - e)

            @pl.when(j + e < fast)
            def _():
                arrive(h, k * fast + j + e)
                if fast > 2:
                    send((3,), h, k * fast + j + e)
            return carry
        lax.fori_loop(1, fast, body, 0)

    def accumulate(h, k, first_row, row_count, fresh):
        columns = pl.ds(pl.multiple_of(k * group_rows, group_rows), group_rows)

        def body(b, carry):
            at = pl.ds(pl.multiple_of(first_row + b * ROW_BLOCK, ROW_BLOCK), ROW_BLOCK)
            product = jnp.dot(
                clip_buf[at, columns], weight_buf[h, columns, :],
                preferred_element_type=jnp.float32,
            )
            if fresh:
                total[h, at, :] = product
            else:
                total[h, at, :] += product
            return carry
        lax.fori_loop(0, row_count // ROW_BLOCK, body, 0)

    def fast_step(h, d, row_count):
        if d == 0:
            fast_line(h, i)
            accumulate(h, i, 0, row_count, True)
            return

        @pl.when(i - d >= 0)
        def _():
            fast_line(h, i - d)
            accumulate(h, i - d, 0, row_count, False)

        @pl.when(i + d < slow)
        def _():
            fast_line(h, i + d)
            accumulate(h, i + d, 0, row_count, False)

    def out_copy(way, h):
        clip = 0 if way == 0 else 1
        part = c if way == 1 else 1 - c
        device = (sibling, peer, cross)[way]
        column = ((2 * c + x) * heads + h) * HEAD
        return pltpu.make_async_remote_copy(
            src_ref=out_buf.at[clip, h, pl.ds(pl.multiple_of(part * half, half), half), :],
            dst_ref=out.at[0, :, pl.ds(pl.multiple_of(column, HEAD), HEAD)],
            send_sem=out_send.at[way, h], recv_sem=out_recv.at[way, h],
            device_id=device, device_id_type=MESH,
        )

    def out_arrived(way, h):
        source_x, source_c = ((x, 1 - c), (1 - x, c), (1 - x, 1 - c))[way]
        column = ((2 * source_c + source_x) * heads + h) * HEAD
        pltpu.make_async_remote_copy(
            src_ref=out_buf.at[0, h, pl.ds(0, half), :],
            dst_ref=out.at[0, :, pl.ds(pl.multiple_of(column, HEAD), HEAD)],
            send_sem=out_send.at[way, h], recv_sem=out_recv.at[way, h],
            device_id=(sibling, peer, cross)[way], device_id_type=MESH,
        ).wait_recv()

    def out_own(h):
        column = ((2 * c + x) * heads + h) * HEAD
        return pltpu.make_async_copy(
            out_buf.at[0, h, pl.ds(pl.multiple_of(c * half, half), half), :],
            out.at[0, :, pl.ds(pl.multiple_of(column, HEAD), HEAD)],
            out_local.at[h],
        )

    def head_norm(block, gain_row):
        scale = lax.rsqrt(jnp.mean(block * block, axis=-1, keepdims=True) + 1e-06)
        return (block * scale * gain_row).astype(jnp.bfloat16)

    exponent = math.log2(math.e) / math.sqrt(HEAD)

    def attend(clip, h):
        query_gain = gain[0:1, head_columns(h)]
        key_gain = gain[1:2, head_columns(h)]

        def prepare(b, carry):
            at = pl.ds(pl.multiple_of(b * ROW_BLOCK, ROW_BLOCK), ROW_BLOCK)
            source = pl.ds(pl.multiple_of(clip * tokens + b * ROW_BLOCK, ROW_BLOCK), ROW_BLOCK)
            key_buf[at, :] = head_norm(total[h, source, HEAD:2 * HEAD], key_gain)
            value_buf[at, :] = total[h, source, 2 * HEAD:].astype(jnp.bfloat16)
            return carry
        lax.fori_loop(0, tokens // ROW_BLOCK, prepare, 0)

        def body(b, carry):
            at = pl.ds(pl.multiple_of(b * ROW_BLOCK, ROW_BLOCK), ROW_BLOCK)
            source = pl.ds(pl.multiple_of(clip * tokens + b * ROW_BLOCK, ROW_BLOCK), ROW_BLOCK)
            queries = head_norm(total[h, source, 0:HEAD], query_gain)
            scores = lax.dot_general(
                queries, key_buf[...], (((1,), (1,)), ((), ())),
                preferred_element_type=jnp.float32,
            )
            most = jnp.max(scores, axis=-1, keepdims=True)
            weights = jnp.exp2((scores - most) * exponent)
            share = 1.0 / jnp.sum(weights, axis=-1, keepdims=True)
            probs = (weights * share).astype(jnp.bfloat16)
            out_buf[clip, h, at, :] = jnp.dot(
                probs, value_buf[...], preferred_element_type=jnp.float32
            ).astype(jnp.bfloat16)
            return carry
        lax.fori_loop(0, tokens // ROW_BLOCK, body, 0)

        if clip == 0:
            out_copy(0, h).start()
            out_own(h).start()
        else:
            out_copy(1, h).start()
            out_copy(2, h).start()

    send((0, 1, 2, 3), 0, f)
    for k in range(min(2, slow)):
        peer_copy(k).start()
    for k in range(slow):
        own_copy(k).start()
        sib_copy(k).start()
    for h in range(1, heads):
        merge(h)

    last = heads - 1
    for t in range(heads * slow + 1):
        h, d = divmod(t, slow)
        if t < heads * slow and d > 0:
            slow_step(h, d)
        if (t + 2) % slow == 0 and 1 <= (t + 2) // slow <= last:
            send((0, 1, 2, 3), (t + 2) // slow, f)
        if t >= 2 and t % 2 == 0 and (t - 2) // 2 < slow:
            k = (t - 2) // 2
            peer_copy(k).wait()
            if k + 2 < slow:
                peer_copy(k + 2).start()
            fwd_copy(k).start()
        if t == slow + 1:
            for k in range(slow):
                if 2 * k + 3 <= slow:
                    accumulate(0, k, tokens, tokens, k == 0)
        if t >= 3 and t % 2 == 1 and (t - 3) // 2 < slow:
            k = (t - 3) // 2
            fwd_copy(k).wait()
            if t > slow:
                accumulate(0, k, tokens, tokens, k == 0)
        if t == 1:
            for k in range(slow):
                own_copy(k).wait()
                sib_copy(k).wait()
        if t >= 1:
            h, d = divmod(t - 1, slow)
            fast_step(h, d, 2 * tokens if h == last else tokens)
            if d == slow - 1 and h < last:
                attend(0, h)
        if t == 2 * slow + 1:
            attend(1, 0)
        if t == 2 * slow + 2:
            for k in range(slow):
                accumulate(1, k, tokens, tokens, k == 0)
            attend(1, 1)

    attend(1, last)
    attend(0, last)

    for h in range(heads):
        def sent(shard, carry, h=h):
            k, jj = lax.div(shard, fast), lax.rem(shard, fast)
            mine = jj == j
            for way, which in (
                (0, mine & (k <= i)), (1, mine & (k >= i)), (2, jj <= j), (3, jj >= j)
            ):
                @pl.when(steps[way][1] & which)
                def _(way=way):
                    weight_copy(way, h, shard).wait_send()
            return carry
        lax.fori_loop(0, slow * fast, sent, 0)
        out_own(h).wait()
        for way in range(3):
            out_copy(way, h).wait_send()
            out_arrived(way, h)


def per_device(
    devices, frames, frozen_query_key_value, adapter_down_weight, adapter_up_weight,
    query_key_norm_gain,
):
    slow, fast = line_shape(devices)
    _, half, _ = frames.shape
    _, rows, columns = frozen_query_key_value.shape
    heads = columns // HEAD // 2
    depth = rows * devices
    wide = 3 * HEAD
    dma = pltpu.SemaphoreType.DMA
    vmem = pl.BlockSpec(memory_space=pltpu.VMEM)
    hbm = pl.BlockSpec(memory_space=pl.ANY)
    return pl.pallas_call(
        functools.partial(kernel, slow, fast, heads),
        out_shape=jax.ShapeDtypeStruct((1, half, 2 * columns), jnp.bfloat16),
        in_specs=[hbm, vmem, vmem, vmem, vmem],
        out_specs=hbm,
        scratch_shapes=[
            pltpu.VMEM((4 * half, depth), jnp.bfloat16),
            pltpu.VMEM((heads, depth, wide), jnp.bfloat16),
            pltpu.VMEM((heads, 4 * half, wide), jnp.float32),
            pltpu.VMEM((2, heads, 2 * half, HEAD), jnp.bfloat16),
            pltpu.VMEM((2 * half, HEAD), jnp.bfloat16),
            pltpu.VMEM((2 * half, HEAD), jnp.bfloat16),
            dma((4, heads, devices)),
            dma((heads, devices)),
            dma((slow,)), dma((slow,)), dma((slow,)), dma((slow,)), dma((slow,)), dma((slow,)),
            dma((slow,)),
            dma((3, heads)), dma((3, heads)), dma((heads,)),
        ],
        compiler_params=pltpu.CompilerParams(
            collective_id=0, has_side_effects=True, vmem_limit_bytes=56 * 1024 * 1024
        ),
    )(
        frames, frozen_query_key_value, adapter_down_weight, adapter_up_weight,
        query_key_norm_gain,
    )


def solution(mesh):
    placed = (
        P(("groups", "fsdp"), "seq", None),
        P(None, "fsdp", "seq"),
        P(None, "fsdp", None),
        P(None, None, "seq"),
        P(None, "seq"),
    )
    return jax.shard_map(
        functools.partial(per_device, mesh.shape["fsdp"]),
        mesh=mesh,
        in_specs=placed,
        out_specs=P(("groups", "fsdp"), "seq", None),
        check_vma=False,
    )
```

time: 280 us -> 111 us (0.40)
  waiting for transfers between devices: 214 us -> 0 us
  Pallas kernels: 0 us -> 107 us
  matrix products: 33.1 us -> 0 us
  between operations: 13.5 us -> 0.01 us
  local copies, waits for them, and re-layouts: 12.6 us -> 4.16 us
  blocking collectives: 4.68 us -> 0 us
    all_gather x2 -> x0, waiting for transfers between devices: 213 us -> none  [the longest x1 199 us: per_device(): combined_weight = lax.all_gather(merged_local, 'fsdp', axis=1, tiled=True)]
    pallas_call x0 -> x1, Pallas kernels: none -> 107 us  [per_device(): pl.pallas_call(functools.partial(kernel, slow, fast, heads), out_shape=ja...]
    dot_general x3 -> x0, matrix products: 23.4 us -> none  [the longest x1 15.4 us: per_device(): jnp.einsum('tn,pnc->ptc', clip_rows, combined_weight, preferred_element_t...]
    sub x1 -> x0, matrix products: 9.65 us -> none  [attend(): probs = jax.nn.softmax(scores, axis=-1).astype(jnp.bfloat16)]
    squeeze x2 -> x0, local copies, waits for them, and re-layouts: 5.06 us -> none  [the longest x1 3.06 us: attend(): queries = head_norm(split_heads[0], gains[0])]
    all_to_all x1 -> x0, blocking collectives: 4.68 us -> none  [per_device(): lax.all_to_all(head_major, 'seq', split_axis=0, concat_axis=1, tiled=True)]
    slice x3 -> x0, local copies, waits for them, and re-layouts: 2.87 us -> none  [the longest x2 1.74 us: attend(): key_rows = head_norm(split_heads[1], gains[1])]
  transfers between devices with their start and end apart: 2 -> 0, of which waited for: 2 -> 0; matrix products, arithmetic and copies ran while one was open for 2% -> 0% of each run, Pallas kernels for 0% -> 0%
where the time goes in v1:
time: 111 us
  Pallas kernels  107 us (96%)
  local copies, waits for them, and re-layouts  4.16 us (4%)
    pallas_call x1, Pallas kernels, per_device(): pl.pallas_call(functools.partial(kernel, slow, fast, heads), out_shape=ja...  107 us
    unnamed x2, local copies, waits for them, and re-layouts  4.16 us

profile of v1, /device:TPU:0, one launch (start us, length us, event | category | flops | bytes accessed | tf_op | source)
XLA Modules:
  0.0 111.2 jit_solution(17658937827307558416)
XLA Ops:
  0.0 1.8 %copy.6.down = bf16[3,384,64]{2,1,0:T(8,128)(2,1)} copy(bf16[3,384,64]{1,2,0:T(8,128)(2,1)} %param.7) | data formatting | bytes 294912 | tf_op args[2]
  1.8 107.1 %shard_map.55 = bf16[1,384,1536]{2,1,0:T(8,128)(2,1)} custom-call(bf16[1,384,3072]{2,1,0:T(8,128)(2,1)} %frames.1, bf16[3,384,768]{2,1,0:T(8,128)(2,1)} %frozen.1, bf16[3,384,64]{2,1,0:T(8,128)(2,1)} %copy.6.down, bf16[3,64,768]{2,1,0:T(8,128)(2,1)} %up.1, f32[2,768]{1,0:T(2,128)} %gain.1), custom_call_target="tpu_custom_call" | custom-call | tf_op jit(solution)/shard_map/pallas_call | solution.py:341
  108.9 2.4 %copy.8 = bf16[1,384,1536]{2,1,0:T(8,128)(2,1)} copy(bf16[1,384,1536]{2,1,0:T(8,128)(2,1)} %shard_map.55) | data formatting | bytes 2359296

commit v2 on v1

--- a/solution.py
+++ b/solution.py
@@ -12,6 +12,7 @@
 MESH = pl.DeviceIdType.MESH
 adapter_scale = 0.5
 ROW_BLOCK = 256
+PARTS = 2
 
 
 def line_shape(devices):
@@ -25,8 +26,8 @@
     slow, fast, heads,
     frames, frozen, down, up, gain,
     out,
-    clip_buf, weight_buf, total, out_buf, key_buf, value_buf,
-    weight_send, weight_recv,
+    clip_buf, weight_buf, total, out_buf, key_buf, value_buf, frozen_buf,
+    weight_send, weight_recv, side_send, side_recv, frozen_sem,
     peer_send, peer_recv, sib_send, sib_recv, fwd_send, fwd_recv, own_sem,
     out_send, out_recv, out_local,
 ):
@@ -36,6 +37,7 @@
     half = frames.shape[1]
     tokens = 2 * half
     group_rows = fast * rows
+    side_rows = max(16, rows // 96 * 16)
     sibling, peer, cross = (x, f, 1 - c), (1 - x, f, c), (1 - x, f, 1 - c)
     steps = {
         0: ((x, f + fast, c), i + 1 < slow),
@@ -44,6 +46,12 @@
         3: ((x, f - 1, c), j > 0),
     }
 
+    own_heads = pltpu.make_async_copy(
+        frozen.at[:, :, pl.ds(pl.multiple_of(heads * x * HEAD, HEAD), heads * HEAD)],
+        frozen_buf, frozen_sem,
+    )
+    own_heads.start()
+
     barrier = pltpu.get_barrier_semaphore()
     for device in (sibling, peer, cross):
         pl.semaphore_signal(barrier, inc=1, device_id=device, device_id_type=MESH)
@@ -60,15 +68,18 @@
 
     def merge(h):
         for p in range(3):
-            product = jnp.dot(
-                down[p], up[p, :, head_columns(h)], preferred_element_type=jnp.float32
+            product = lax.dot_general(
+                down[p], up[p, :, head_columns(h)], (((0,), (0,)), ((), ())),
+                preferred_element_type=jnp.float32,
             )
-            merged = frozen[p, :, head_columns(h)].astype(jnp.float32) + adapter_scale * product
+            merged = (
+                frozen_buf[p, :, h * HEAD:(h + 1) * HEAD].astype(jnp.float32)
+                + adapter_scale * product
+            )
             weight_buf[h, pl.ds(pl.multiple_of(f * rows, rows), rows), p * HEAD:(p + 1) * HEAD] = (
                 merged.astype(jnp.bfloat16)
             )
 
-    merge(0)
     pl.semaphore_wait(barrier, expected)
 
     def chunk(k):
@@ -106,49 +117,67 @@
             device_id=sibling, device_id_type=MESH,
         )
 
-    def weight_copy(way, h, shard):
-        block = weight_buf.at[h, pl.ds(pl.multiple_of(shard * rows, rows), rows), :]
+    def weight_copy(way, h, shard, main=False):
+        first, count = (side_rows, rows - side_rows) if main else (0, rows)
+        block = weight_buf.at[h, pl.ds(pl.multiple_of(shard * rows + first, 16), count), :]
         return pltpu.make_async_remote_copy(
             src_ref=block, dst_ref=block,
             send_sem=weight_send.at[way, h, shard], recv_sem=weight_recv.at[h, shard],
             device_id=steps[way][0], device_id_type=MESH,
         )
 
-    def send(ways, h, shard):
+    def side_copy(way, h, shard):
+        block = weight_buf.at[h, pl.ds(pl.multiple_of(shard * rows, 16), side_rows), :]
+        return pltpu.make_async_remote_copy(
+            src_ref=block, dst_ref=block,
+            send_sem=side_send.at[way, h, shard], recv_sem=side_recv.at[h, shard],
+            device_id=steps[way][0], device_id_type=MESH,
+        )
+
+    def send(ways, h, shard, main=False):
         for way in ways:
             @pl.when(steps[way][1])
             def _(way=way):
-                weight_copy(way, h, shard).start()
-
-    def arrive(h, shard):
-        weight_copy(0, h, shard).wait_recv()
+                weight_copy(way, h, shard, main).start()
+
+    def send_side(ways, h, shard):
+        for way in ways:
+            @pl.when(steps[way][1])
+            def _(way=way):
+                side_copy(way, h, shard).start()
+
+    def arrive(h, shard, main=False):
+        weight_copy(0, h, shard, main).wait_recv()
 
     def slow_step(h, d):
         @pl.when(i - d >= 0)
         def _():
             shard = (i - d) * fast + j
             arrive(h, shard)
-            send((0, 2, 3), h, shard)
+            send((0,), h, shard)
+            send((2, 3), h, shard, True)
 
         @pl.when(i + d < slow)
         def _():
             shard = (i + d) * fast + j
             arrive(h, shard)
-            send((1, 2, 3), h, shard)
-
-    def fast_line(h, k):
+            send((1,), h, shard)
+            send((2, 3), h, shard, True)
+
+    def fast_line(h, k, ways):
+        own = len(ways) == 2
+
         def body(e, carry):
-            @pl.when(j - e >= 0)
-            def _():
-                arrive(h, k * fast + j - e)
-                if fast > 2:
-                    send((2,), h, k * fast + j - e)
-
-            @pl.when(j + e < fast)
-            def _():
-                arrive(h, k * fast + j + e)
-                if fast > 2:
-                    send((3,), h, k * fast + j + e)
+            for jj, there, way in ((j - e, j - e >= 0, 2), (j + e, j + e < fast, 3)):
+                @pl.when(there)
+                def _(jj=jj, way=way):
+                    shard = k * fast + jj
+                    arrive(h, shard, not own)
+                    if fast > 2:
+                        send((way,), h, shard, not own)
+                    if not own:
+                        side_copy(0, h, shard).wait_recv()
+                    send_side(ways, h, shard)
             return carry
         lax.fori_loop(1, fast, body, 0)
 
@@ -170,18 +199,18 @@
 
     def fast_step(h, d, row_count):
         if d == 0:
-            fast_line(h, i)
+            fast_line(h, i, (0, 1))
             accumulate(h, i, 0, row_count, True)
             return
 
         @pl.when(i - d >= 0)
         def _():
-            fast_line(h, i - d)
+            fast_line(h, i - d, (0,))
             accumulate(h, i - d, 0, row_count, False)
 
         @pl.when(i + d < slow)
         def _():
-            fast_line(h, i + d)
+            fast_line(h, i + d, (1,))
             accumulate(h, i + d, 0, row_count, False)
 
     def out_copy(way, h):
@@ -232,34 +261,35 @@
             return carry
         lax.fori_loop(0, tokens // ROW_BLOCK, prepare, 0)
 
-        def body(b, carry):
-            at = pl.ds(pl.multiple_of(b * ROW_BLOCK, ROW_BLOCK), ROW_BLOCK)
-            source = pl.ds(pl.multiple_of(clip * tokens + b * ROW_BLOCK, ROW_BLOCK), ROW_BLOCK)
-            queries = head_norm(total[h, source, 0:HEAD], query_gain)
-            scores = lax.dot_general(
-                queries, key_buf[...], (((1,), (1,)), ((), ())),
-                preferred_element_type=jnp.float32,
-            )
-            most = jnp.max(scores, axis=-1, keepdims=True)
-            weights = jnp.exp2((scores - most) * exponent)
-            share = 1.0 / jnp.sum(weights, axis=-1, keepdims=True)
-            probs = (weights * share).astype(jnp.bfloat16)
-            out_buf[clip, h, at, :] = jnp.dot(
-                probs, value_buf[...], preferred_element_type=jnp.float32
-            ).astype(jnp.bfloat16)
-            return carry
-        lax.fori_loop(0, tokens // ROW_BLOCK, body, 0)
-
-        if clip == 0:
-            out_copy(0, h).start()
-            out_own(h).start()
-        else:
-            out_copy(1, h).start()
-            out_copy(2, h).start()
-
-    send((0, 1, 2, 3), 0, f)
+        for part in (1 - c, c):
+            for b in range(PARTS):
+                size = half // PARTS
+                at = pl.ds(pl.multiple_of(part * half + b * size, size), size)
+                source = pl.ds(pl.multiple_of(clip * tokens + part * half + b * size, size), size)
+                queries = head_norm(total[h, source, 0:HEAD], query_gain)
+                scores = lax.dot_general(
+                    queries, key_buf[...], (((1,), (1,)), ((), ())),
+                    preferred_element_type=jnp.float32,
+                )
+                most = jnp.max(scores, axis=-1, keepdims=True)
+                weights = jnp.exp2((scores - most) * exponent)
+                share = 1.0 / jnp.sum(weights, axis=-1, keepdims=True)
+                probs = (weights * share).astype(jnp.bfloat16)
+                out_buf[clip, h, at, :] = jnp.dot(
+                    probs, value_buf[...], preferred_element_type=jnp.float32
+                ).astype(jnp.bfloat16)
+            if clip == 1:
+                out_copy(1 if part is c else 2, h).start()
+            elif part is c:
+                out_own(h).start()
+            else:
+                out_copy(0, h).start()
+
     for k in range(min(2, slow)):
         peer_copy(k).start()
+    own_heads.wait()
+    merge(0)
+    send((0, 1, 2, 3), 0, f)
     for k in range(slow):
         own_copy(k).start()
         sib_copy(k).start()
@@ -271,8 +301,8 @@
         h, d = divmod(t, slow)
         if t < heads * slow and d > 0:
             slow_step(h, d)
-        if (t + 2) % slow == 0 and 1 <= (t + 2) // slow <= last:
-            send((0, 1, 2, 3), (t + 2) // slow, f)
+        if t % slow == 1 and t // slow < last:
+            send((0, 1, 2, 3), t // slow + 1, f)
         if t >= 2 and t % 2 == 0 and (t - 2) // 2 < slow:
             k = (t - 2) // 2
             peer_copy(k).wait()
@@ -310,13 +340,22 @@
     for h in range(heads):
         def sent(shard, carry, h=h):
             k, jj = lax.div(shard, fast), lax.rem(shard, fast)
-            mine = jj == j
-            for way, which in (
-                (0, mine & (k <= i)), (1, mine & (k >= i)), (2, jj <= j), (3, jj >= j)
-            ):
-                @pl.when(steps[way][1] & which)
+            for way, passes in ((0, k <= i), (1, k >= i)):
+                @pl.when(steps[way][1] & passes & (jj == j))
                 def _(way=way):
                     weight_copy(way, h, shard).wait_send()
+
+                @pl.when(steps[way][1] & passes & (jj != j))
+                def _(way=way):
+                    side_copy(way, h, shard).wait_send()
+            for way, passes in ((2, jj <= j), (3, jj >= j)):
+                @pl.when(steps[way][1] & passes & (k == i))
+                def _(way=way):
+                    weight_copy(way, h, shard).wait_send()
+
+                @pl.when(steps[way][1] & passes & (k != i))
+                def _(way=way):
+                    weight_copy(way, h, shard, True).wait_send()
             return carry
         lax.fori_loop(0, slow * fast, sent, 0)
         out_own(h).wait()
@@ -341,7 +380,7 @@
     return pl.pallas_call(
         functools.partial(kernel, slow, fast, heads),
         out_shape=jax.ShapeDtypeStruct((1, half, 2 * columns), jnp.bfloat16),
-        in_specs=[hbm, vmem, vmem, vmem, vmem],
+        in_specs=[hbm, hbm, vmem, vmem, vmem],
         out_specs=hbm,
         scratch_shapes=[
             pltpu.VMEM((4 * half, depth), jnp.bfloat16),
@@ -350,8 +389,12 @@
             pltpu.VMEM((2, heads, 2 * half, HEAD), jnp.bfloat16),
             pltpu.VMEM((2 * half, HEAD), jnp.bfloat16),
             pltpu.VMEM((2 * half, HEAD), jnp.bfloat16),
+            pltpu.VMEM((3, rows, heads * HEAD), jnp.bfloat16),
             dma((4, heads, devices)),
             dma((heads, devices)),
+            dma((2, heads, devices)),
+            dma((heads, devices)),
+            dma,
             dma((slow,)), dma((slow,)), dma((slow,)), dma((slow,)), dma((slow,)), dma((slow,)),
             dma((slow,)),
             dma((3, heads)), dma((3, heads)), dma((heads,)),
@@ -360,8 +403,8 @@
             collective_id=0, has_side_effects=True, vmem_limit_bytes=56 * 1024 * 1024
         ),
     )(
-        frames, frozen_query_key_value, adapter_down_weight, adapter_up_weight,
-        query_key_norm_gain,
+        frames, frozen_query_key_value, jnp.swapaxes(adapter_down_weight, 1, 2),
+        adapter_up_weight, query_key_norm_gain,
     )
 
 

time: 111 us -> 106 us (0.955)
  Pallas kernels: 107 us -> 104 us
  local copies, waits for them, and re-layouts: 4.16 us -> 2.36 us
    pallas_call x1, Pallas kernels: 107 us -> 104 us  [per_device(): pl.pallas_call(functools.partial(kernel, slow, fast, heads), out_shape=ja...]
    unnamed x2 -> x1, local copies, waits for them, and re-layouts: 4.16 us -> 2.36 us
where the time goes in v2:
time: 106 us
  Pallas kernels  104 us (98%)
  local copies, waits for them, and re-layouts  2.36 us (2%)
    pallas_call x1, Pallas kernels, per_device(): pl.pallas_call(functools.partial(kernel, slow, fast, heads), out_shape=ja...  104 us
    unnamed x1, local copies, waits for them, and re-layouts  2.36 us

profile of v2, /device:TPU:0, one launch (start us, length us, event | category | flops | bytes accessed | tf_op | source)
XLA Modules:
  0.0 106.2 jit_solution(6084311106346318923)
XLA Ops:
  0.0 103.8 %shard_map.55 = bf16[1,384,1536]{2,1,0:T(8,128)(2,1)} custom-call(bf16[1,384,3072]{2,1,0:T(8,128)(2,1)} %frames.1, bf16[3,384,768]{2,1,0:T(8,128)(2,1)} %frozen.1, bf16[3,64,384]{2,1,0:T(8,128)(2,1)} %bitcast.1, bf16[3,64,768]{2,1,0:T(8,128)(2,1)} %up.1, f32[2,768]{1,0:T(2,128)} %gain.1), custom_call_target="tpu_custom_call" | custom-call | tf_op jit(solution)/shard_map/pallas_call | solution.py:380
  103.8 2.4 %copy.7 = bf16[1,384,1536]{2,1,0:T(8,128)(2,1)} copy(bf16[1,384,1536]{2,1,0:T(8,128)(2,1)} %shard_map.55) | data formatting | bytes 2359296
